TPU v7x, 128 devices: a whole 4x4x4 slice. The times are simulated.
128 devices in a mesh: work: 128 (over x, y, z, core).
Axes of the slice: x: 4, y: 4, z: 4, core: 2. Of those that a mesh axis runs over, the one named last changes fastest.
Arguments:
- embeddings: bfloat16 [65536, 1024], P('work'), may hold values from -6 to 6
- labels: int32 [65536, 1], P('work'), may hold values from 0 to 255; in each aligned block of 512 rows (0 to 511, 512 to 1023, ...) at most 4 rows name the same one
Outputs:
- nearest: float32 [65536], P('work')
Inputs may be any that keep to these rules, and one draw needn't show every extreme that they name: `labels`: within the rows of one device no label occurs more than 4 times, and in every draw some label occurs exactly 4 times on some device; every label occurs somewhere.
All inputs are finite; a program needn't handle non-finite values.
Results may differ from a plain program's by a relative error of at most 0.0015.
Values may be sent and summed in bfloat16 or wider, within the bound.
No kernel may reach another device: no remote copies, remote signals or barrier semaphores. Data moves between devices by JAX's collectives and lax.ppermute only.
A program may use at most 64 MiB of HBM per device.

v0:
```python
import jax
import jax.numpy as jnp
from jax import lax
from jax.sharding import PartitionSpec as P

CL_DEV = 2


def cluster_maxima(pieces):
    rows, flags = pieces
    count = rows.shape[0]
    owned = rows.shape[1]
    most = rows.shape[2]
    width = rows.shape[3]
    size = count * most
    grouped = jnp.transpose(rows, (1, 0, 2, 3)).reshape(owned, size, width)
    live = jnp.transpose(flags, (1, 0, 2)).reshape(owned, size) > 0.5
    step_rows = 512
    step_rows = min(step_rows, size)
    places = jnp.arange(size, dtype=jnp.int32)

    def slot_block(index):
        first = index * step_rows
        sim = jnp.einsum("cid,cjd->cij", grouped, grouped, preferred_element_type=jnp.float32)
        query_pos = first + jnp.arange(step_rows, dtype=jnp.int32)
        usable = live[:, None, :] & (query_pos[:, None] != places[None, :])[None, :, :]
        return jnp.max(jnp.where(usable, sim, jnp.float32(-1.0)), axis=2)

    blocks = lax.map(slot_block, jnp.arange(size // step_rows, dtype=jnp.int32))
    best = jnp.transpose(blocks, (1, 0, 2)).reshape(owned, size)
    best = jnp.transpose(best.reshape(owned, count, most), (1, 0, 2))
    return lax.all_to_all(best, "work", split_axis=0, concat_axis=0, tiled=True)


def local(embeddings, labels):
    count = lax.axis_size("work")
    row_count = embeddings.shape[0]
    width = embeddings.shape[1]
    most = 2 * row_count // (CL_DEV * count)
    label_row = labels[:, 0]
    values = embeddings.astype(jnp.float32)
    squares = jnp.sum(values * values, axis=1, keepdims=True)
    unit = (values * lax.rsqrt(squares + 1e-06)).astype(jnp.bfloat16)
    places = jnp.arange(row_count, dtype=jnp.int32)
    earlier = (label_row[:, None] == label_row[None, :]) & (places[:, None] > places[None, :])
    rank = jnp.sum(earlier.astype(jnp.int32), axis=1)
    slot = label_row * most + rank
    total = CL_DEV * count * most
    send_rows = (
        jnp.zeros((total, width), jnp.bfloat16)
        .at[slot]
        .set(unit)
        .reshape(count, CL_DEV, most, width)
    )
    send_flags = (
        jnp.zeros((total,), jnp.bfloat16)
        .at[slot]
        .set(jnp.bfloat16(1.0))
        .reshape(count, CL_DEV, most)
    )
    result = cluster_maxima(
        (
            lax.all_to_all(send_rows, "work", split_axis=0, concat_axis=0, tiled=True),
            lax.all_to_all(send_flags, "work", split_axis=0, concat_axis=0, tiled=True),
        )
    )
    flat = result.reshape(total)
    return flat[slot]


def solution(mesh):
    return jax.shard_map(
        local,
        mesh=mesh,
        in_specs=(P("work", None), P("work", None)),
        out_specs=P("work"),
        check_vma=False,
    )
```

profile of v0, /device:TPU:1, one launch (start us, length us, event | category | flops | bytes accessed | tf_op | source)
XLA Modules:
  0.0 90.7 jit_solution(3223824767517039668)
XLA Ops:
  0.0 1.0 %convert_reduce_fusion = s32[512]{0:T(512)S(1)} fusion(s32[512]{0:T(512)} %bitcast.11), kind=kLoop, calls=%fused_computation.12 | loop fusion | flops 1310208 | bytes 4096 | tf_op jit(solution)/shard_map/reduce_sum | solution.py:46
  1.0 0.7 compare_select_fusion
  1.7 3.8 %scatter_custom_fusion = bf16[1024]{0:T(1024)(128)(2,1)S(1)} fusion(s32[512]{0:T(512)S(1)} %bitcast.12, bf16[512]{0:T(512)(128)(2,1)S(1)} %broadcast.31, bf16[]{:T(256)} %constant.10.clone.1), kind=kCustom, calls=%fused_computation.19 | custom fusion | bytes 2050 | tf_op jit(solution)/shard_map/scatter | solution.py:58
  5.5 0.8 reshape.46
  6.2 11.5 %all-to-all-start = ((bf16[128,2,4]{2,1,0:T(2,128)(2,1)}), bf16[128,2,4]{2,1,0:T(2,128)(2,1)S(1)}, u32[]{:S(2)}, u32[]{:S(2)}) async-start(bf16[128,2,4]{2,1,0:T(2,128)(2,1)} %reshape.46), calls=%async_computation | async-start | bytes 131072 | tf_op jit(solution)/shard_map/all_to_all | solution.py:64
  17.8 1.5 %fusion = f32[512]{0:T(512)S(1)} fusion(bf16[512,1024]{1,0:T(8,128)(2,1)} %param.2), kind=kLoop, calls=%fused_computation.5 | loop fusion | flops 1572352 | bytes 1050624 | tf_op jit(solution)/shard_map/reduce_sum | solution.py:42
  19.3 4.0 %scatter_custom_fusion.1 = bf16[1024,1024]{1,0:T(8,128)(2,1)S(1)} fusion(s32[512]{0:T(512)S(1)} %bitcast.13, bf16[512,1024]{1,0:T(8,128)(2,1)} %param.2, f32[512]{0:T(512)S(1)} %add_rsqrt_fusion, bf16[]{:T(256)} %constant.10.clone.1), kind=kCustom, calls=%fused_computation.8 | custom fusion | flops 1572864 | bytes 3147778 | tf_op jit(solution)/shard_map/scatter | solution.py:52
  23.2 2.2 %reshape.47 = bf16[128,2,4,1024]{3,2,1,0:T(4,128)(2,1)} reshape(bf16[1024,1024]{1,0:T(8,128)(2,1)S(1)} %scatter_custom_fusion.1) | data formatting | bytes 4194304 | tf_op jit(solution)/shard_map/reshape | solution.py:53
  25.5 1.6 %all-to-all-done = bf16[128,2,4]{2,1,0:T(2,128)(2,1)S(1)} async-done(((bf16[128,2,4]{2,1,0:T(2,128)(2,1)}), bf16[128,2,4]{2,1,0:T(2,128)(2,1)S(1)}, u32[]{:S(2)}, u32[]{:S(2)}) %all-to-all-start) | async-done | bytes 2080 | tf_op jit(solution)/shard_map/all_to_all | solution.py:64
  27.1 8.1 %all-to-all-start.1 = ((bf16[128,2,4,1024]{3,2,1,0:T(4,128)(2,1)}), bf16[128,2,4,1024]{3,2,1,0:T(4,128)(2,1)S(1)}, u32[]{:S(2)}, u32[]{:S(2)}) async-start(bf16[128,2,4,1024]{3,2,1,0:T(4,128)(2,1)} %reshape.47), calls=%async_computation.1 | async-start | bytes 4194304 | tf_op jit(solution)/shard_map/all_to_all | solution.py:63
  35.2 0.1 iota_compare_fusion
  35.3 0.1 compare_bitcast_fusion
  35.5 0.1 gt.37
  35.6 30.2 %all-to-all-done.1 = bf16[128,2,4,1024]{3,2,1,0:T(4,128)(2,1)S(1)} async-done(((bf16[128,2,4,1024]{3,2,1,0:T(4,128)(2,1)}), bf16[128,2,4,1024]{3,2,1,0:T(4,128)(2,1)S(1)}, u32[]{:S(2)}, u32[]{:S(2)}) %all-to-all-start.1) | async-done | bytes 2097184 | tf_op jit(solution)/shard_map/all_to_all | solution.py:63
  65.8 2.1 %copy.10 = bf16[2,128,4,1024]{3,2,1,0:T(4,128)(2,1)} copy(bf16[2,128,4,1024]{3,2,0,1:T(4,128)(2,1)S(1)} %bitcast.9) | data formatting | bytes 4194304 | tf_op jit(solution)/shard_map/transpose | solution.py:16
  67.8 2.5 %reshape.48 = bf16[2,512,1024]{2,1,0:T(8,128)(2,1)S(1)} reshape(bf16[2,128,4,1024]{3,2,1,0:T(4,128)(2,1)} %copy.10) | data formatting | bytes 4194304 | tf_op jit(solution)/shard_map/reshape | solution.py:16
  70.4 1.4 %select_reduce_fusion = f32[2,512]{1,0:T(2,128)S(1)} fusion(bf16[2,512,1024]{2,1,0:T(8,128)(2,1)S(1)} %reshape.48, pred[512,512]{0,1:T(8,128)(4,1)S(1)} %iota_compare_fusion, pred[2,512]{1,0:T(4,128)(4,1)S(1)} %gt.37), kind=kOutput, calls=%fused_computation.7 | convolution fusion | flops 1075313664 | bytes 2364416 | tf_op jit(solution)/shard_map/while/body/eval_jaxpr/cid,cjd->cij/dot_general | solution.py:24
  71.7 0.1 reshape_reshape_transpose.3
  71.9 0.7 copy.11
  72.6 4.6 %all-to-all-start.2 = ((f32[128,2,4]{2,1,0:T(2,128)}), f32[128,2,4]{2,1,0:T(2,128)S(1)}, u32[]{:S(2)}, u32[]{:S(2)}) async-start(f32[128,2,4]{2,1,0:T(2,128)} %copy.11), calls=%async_computation.2 | async-start | bytes 262144 | tf_op jit(solution)/shard_map/all_to_all | solution.py:32
  77.2 9.9 %all-to-all-done.2 = f32[128,2,4]{2,1,0:T(2,128)S(1)} async-done(((f32[128,2,4]{2,1,0:T(2,128)}), f32[128,2,4]{2,1,0:T(2,128)S(1)}, u32[]{:S(2)}, u32[]{:S(2)}) %all-to-all-start.2) | async-done | bytes 4128 | tf_op jit(solution)/shard_map/all_to_all | solution.py:32
  87.1 0.2 reshape.49
  87.3 3.4 %gather_fusion = f32[512]{0:T(512)} fusion(f32[1024]{0:T(1024)S(1)} %reshape.49, s32[1024]{0:T(1024)S(1)} %pad_clamp_fusion), kind=kCustom, calls=%fused_computation | custom fusion | bytes 6144 | tf_op jit(solution)/shard_map/gather | solution.py:68
  (4 shorter events, 0.0 us)
Async XLA Ops:
  6.2 20.9 %all-to-all-start = ((bf16[128,2,4]{2,1,0:T(2,128)(2,1)}), bf16[128,2,4]{2,1,0:T(2,128)(2,1)S(1)}, u32[]{:S(2)}, u32[]{:S(2)}) async-start(bf16[128,2,4]{2,1,0:T(2,128)(2,1)} %reshape.46), calls=%async_computation | async-start | bytes 131072 | tf_op jit(solution)/shard_map/all_to_all | solution.py:64
  27.1 38.7 %all-to-all-start.1 = ((bf16[128,2,4,1024]{3,2,1,0:T(4,128)(2,1)}), bf16[128,2,4,1024]{3,2,1,0:T(4,128)(2,1)S(1)}, u32[]{:S(2)}, u32[]{:S(2)}) async-start(bf16[128,2,4,1024]{3,2,1,0:T(4,128)(2,1)} %reshape.47), calls=%async_computation.1 | async-start | bytes 4194304 | tf_op jit(solution)/shard_map/all_to_all | solution.py:63
  72.6 14.5 %all-to-all-start.2 = ((f32[128,2,4]{2,1,0:T(2,128)}), f32[128,2,4]{2,1,0:T(2,128)S(1)}, u32[]{:S(2)}, u32[]{:S(2)}) async-start(f32[128,2,4]{2,1,0:T(2,128)} %copy.11), calls=%async_computation.2 | async-start | bytes 262144 | tf_op jit(solution)/shard_map/all_to_all | solution.py:32
where the time goes:
time: 91.1 us; the launch traced here: 90.7 us
  waiting for transfers between devices  41.7 us (46%)
  starting transfers between devices  24.2 us (27%)
  local copies, waits for them, and re-layouts  16 us (18%)
  other arithmetic  7.34 us (8%)
  matrix products  1.36 us (1%)
    all_to_all x1, waiting for transfers between devices, local(): lax.all_to_all(send_rows, 'work', split_axis=0, concat_axis=0, tiled=True)  30.2 us
    all_to_all x1, starting transfers between devices, local(): lax.all_to_all(send_flags, 'work', split_axis=0, concat_axis=0, tiled=True)  11.5 us
    all_to_all x1, waiting for transfers between devices, cluster_maxima(): return lax.all_to_all(best, 'work', split_axis=0, concat_axis=0, tiled=True)  9.87 us
    all_to_all x1, starting transfers between devices, local(): lax.all_to_all(send_rows, 'work', split_axis=0, concat_axis=0, tiled=True)  8.14 us
    all_to_all x1, starting transfers between devices, cluster_maxima(): return lax.all_to_all(best, 'work', split_axis=0, concat_axis=0, tiled=True)  4.57 us
    scatter x1, other arithmetic, local(): send_rows = jnp.zeros((total, width), jnp.bfloat16).at[slot].set(unit).re...  3.97 us
    scatter x1, local copies, waits for them, and re-layouts, local(): send_flags = jnp.zeros((total,), jnp.bfloat16).at[slot].set(jnp.bfloat16(...  3.77 us
    gather x1, local copies, waits for them, and re-layouts, local(): return flat[slot]  3.42 us
  transfers between devices with their start and end apart: 3, of which 3 were waited for; matrix products, arithmetic and copies ran while one was open for 9% of the time, Pallas kernels for 0%

commit v1 on v0

v1 whole, which is shorter than its diff:
```python
import jax
import jax.numpy as jnp
from jax import lax
from jax.experimental import pallas as pl
from jax.experimental.pallas import tpu as pltpu
from jax.sharding import PartitionSpec as P

CLUSTERS = 256
CL_DEV = 2
MOST = 4
PART = CL_DEV * MOST
DEAD = 4.0
LOW = -1e30


def iota(shape, dim):
    return lax.broadcasted_iota(jnp.int32, shape, dim)


def parts_of(values):
    out = []
    for _ in range(3):
        part = values.astype(jnp.bfloat16)
        out.append(part)
        values = values - part.astype(jnp.float32)
    return out


def dot(a, b, dims):
    return lax.dot_general(a, b, (dims, ((), ())), preferred_element_type=jnp.float32)


def place_kernel(label_ref, rows_ref, send_ref, slot_ref):
    rows, width = rows_ref.shape
    total = send_ref.shape[0]
    label = label_ref[...]
    member = iota((CLUSTERS, rows), 0) == label
    before = (iota((rows, rows), 0) < iota((rows, rows), 1)).astype(jnp.float32).astype(jnp.bfloat16)
    earlier = dot(member.astype(jnp.float32).astype(jnp.bfloat16), before, ((1,), (0,)))
    rank = jnp.sum(jnp.where(member, earlier, 0.0), axis=0, keepdims=True)
    slot = label * MOST + rank.astype(jnp.int32)
    slot_ref[...] = slot
    values = rows_ref[...].astype(jnp.float32)
    squares = jnp.sum(values * values, axis=1, keepdims=True)
    unit = (values * lax.rsqrt(squares + 1e-06)).astype(jnp.bfloat16)
    step = 256
    for first in range(0, total, step):
        chosen = (iota((step, rows), 0) + first == slot).astype(jnp.float32)
        empty = DEAD - DEAD * jnp.sum(chosen, axis=1, keepdims=True)
        placed = dot(chosen.astype(jnp.bfloat16), unit, ((1,), (0,)))
        send_ref[first : first + step, :128] = (placed[:, :128] + empty).astype(jnp.bfloat16)
        send_ref[first : first + step, 128:] = placed[:, 128:].astype(jnp.bfloat16)


def maxima_kernel(rows_ref, out_ref):
    total = rows_ref.shape[0]
    count = total // PART
    step = 256
    tile = 128
    same = (iota((step, tile), 0) & MOST) == (iota((step, tile), 1) & MOST)
    other = iota((tile, tile), 0) != iota((tile, tile), 1)
    best = jnp.full((8, total), -1.0, jnp.float32)
    for first in range(0, total, step):
        part = rows_ref[first : first + step, :]
        live = part[:, :1].astype(jnp.float32) < 0.5 * DEAD
        bias = jnp.where(same & live, 0.0, LOW)
        sim = dot(part, rows_ref[...], ((1,), (1,)))
        found = []
        for left in range(0, total, tile):
            block = sim[:, left : left + tile] + bias
            if first <= left < first + step:
                top = left - first
                pieces = [block[:top], jnp.where(other, block[top : top + tile], LOW), block[top + tile :]]
                block = jnp.concatenate([p for p in pieces if p.shape[0]], axis=0)
            found.append(jnp.max(block.reshape(step // 8, 8, tile), axis=0))
        best = jnp.maximum(best, jnp.concatenate(found, axis=1))
    best = jnp.max(best, axis=0, keepdims=True)
    mine = iota((count, total), 1) // PART == iota((count, total), 0)
    spread = (iota((total, 128), 0) % PART == iota((total, 128), 1) % PART).astype(jnp.float32).astype(jnp.bfloat16)
    out = jnp.zeros((count, 128), jnp.float32)
    for piece in parts_of(best):
        held = jnp.where(mine, piece.astype(jnp.float32), 0.0).astype(jnp.bfloat16)
        out = out + dot(held, spread, ((1,), (0,)))
    out_ref[...] = out


def lookup_kernel(slot_ref, found_ref, out_ref):
    rows = slot_ref.shape[1]
    count = found_ref.shape[0]
    slot = slot_ref[...]
    owner = (iota((count, rows), 0) == slot // PART).astype(jnp.float32).astype(jnp.bfloat16)
    picked = jnp.zeros((128, rows), jnp.float32)
    for piece in parts_of(found_ref[...]):
        picked = picked + dot(piece, owner, ((0,), (0,)))
    picked = picked[:PART]
    out_ref[...] = jnp.sum(jnp.where(iota((PART, rows), 0) == slot % PART, picked, 0.0), axis=0, keepdims=True)


def call(kernel, out_shape, name):
    return pl.pallas_call(
        kernel,
        out_shape=out_shape,
        compiler_params=pltpu.CompilerParams(vmem_limit_bytes=40 * 1024 * 1024),
        name=name,
    )


def exchange(array):
    return lax.all_to_all(array, "work", split_axis=0, concat_axis=0, tiled=True)


def local(embeddings, labels):
    count = lax.axis_size("work")
    rows, width = embeddings.shape
    total = count * PART
    send, slot = call(
        place_kernel,
        (jax.ShapeDtypeStruct((total, width), jnp.bfloat16), jax.ShapeDtypeStruct((1, rows), jnp.int32)),
        "place",
    )(labels.reshape(1, rows), embeddings)
    held = exchange(send.reshape(count, PART, width)).reshape(total, width)
    best = call(maxima_kernel, jax.ShapeDtypeStruct((count, 128), jnp.float32), "maxima")(held)
    found = exchange(best)
    nearest = call(lookup_kernel, jax.ShapeDtypeStruct((1, rows), jnp.float32), "lookup")(slot, found)
    return nearest.reshape(rows)


def solution(mesh):
    return jax.shard_map(
        local,
        mesh=mesh,
        in_specs=(P("work", None), P("work", None)),
        out_specs=P("work"),
        check_vma=False,
    )
```

time: 91.1 us -> 62.8 us (0.69)
  blocking collectives: 0 us -> 55.2 us
  waiting for transfers between devices: 41.7 us -> 0 us
  starting transfers between devices: 24.2 us -> 0 us
  local copies, waits for them, and re-layouts: 16 us -> 1.91 us
  other arithmetic: 7.34 us -> 0 us
  Pallas kernels: 0 us -> 5.44 us
  matrix products: 1.36 us -> 0 us
    all_to_all x0 -> x2, blocking collectives: none -> 55.2 us  [exchange(): lax.all_to_all(array, 'work', split_axis=0, concat_axis=0, tiled=True)]
    all_to_all x3 -> x0, waiting for transfers between devices: 41.7 us -> none  [the longest x1 30.2 us: local(): lax.all_to_all(send_rows, 'work', split_axis=0, concat_axis=0, tiled=True)]
    all_to_all x3 -> x0, starting transfers between devices: 24.2 us -> none  [the longest x1 11.5 us: local(): lax.all_to_all(send_flags, 'work', split_axis=0, concat_axis=0, tiled=True)]
    reshape x4 -> x0, local copies, waits for them, and re-layouts: 5.73 us -> none  [the longest x1 2.54 us: cluster_maxima(): grouped = jnp.transpose(rows, (1, 0, 2, 3)).reshape(owned, size, width)]
    pallas_call x0 -> x3, Pallas kernels: none -> 5.44 us  [the longest x1 2.7 us: local(): call(maxima_kernel, jax.ShapeDtypeStruct((count, 128), jnp.float32), 'max...]
    scatter x1 -> x0, other arithmetic: 3.97 us -> none  [local(): send_rows = jnp.zeros((total, width), jnp.bfloat16).at[slot].set(unit).re...]
    scatter x1 -> x0, local copies, waits for them, and re-layouts: 3.77 us -> none  [local(): send_flags = jnp.zeros((total,), jnp.bfloat16).at[slot].set(jnp.bfloat16(...]
    gather x1 -> x0, local copies, waits for them, and re-layouts: 3.42 us -> none  [local(): return flat[slot]]
  transfers between devices with their start and end apart: 3 -> 0, of which waited for: 3 -> 0; matrix products, arithmetic and copies ran while one was open for 9% -> 0% of each run, Pallas kernels for 0% -> 0%
where the time goes in v1:
time: 62.8 us; the launch traced here: 62.6 us
  blocking collectives  55.2 us (88%)
  Pallas kernels  5.44 us (9%)
  local copies, waits for them, and re-layouts  1.91 us (3%)
    all_to_all x2, blocking collectives, exchange(): lax.all_to_all(array, 'work', split_axis=0, concat_axis=0, tiled=True)  55.2 us
    pallas_call x1, Pallas kernels, local(): call(maxima_kernel, jax.ShapeDtypeStruct((count, 128), jnp.float32), 'max...  2.7 us
    unnamed x4, local copies, waits for them, and re-layouts  1.91 us
    pallas_call x1, Pallas kernels, local(): call(place_kernel, (jax.ShapeDtypeStruct((total, width), jnp.bfloat16), j...  1.89 us

profile of v1, /device:TPU:1, one launch (start us, length us, event | category | flops | bytes accessed | tf_op | source)
XLA Modules:
  0.0 62.6 jit_solution(2873955217616059622)
XLA Ops:
  0.0 0.0 copy-start
  0.0 1.2 %copy-done = bf16[512,1024]{1,0:T(8,128)(2,1)S(1)} copy-done((bf16[512,1024]{1,0:T(8,128)(2,1)S(1)}, bf16[512,1024]{1,0:T(8,128)(2,1)}, u32[]{:S(2)}) %copy-start) | copy-done | bytes 1048600
  1.2 0.0 copy-start.1
  1.2 0.7 %copy-done.1 = s32[512,1]{0,1:T(1,128)S(1)} copy-done((s32[512,1]{0,1:T(1,128)S(1)}, s32[512,1]{0,1:T(1,128)}, u32[]{:S(2)}) %copy-start.1) | copy-done | bytes 2072
  1.9 1.9 %place.1 = (bf16[1024,1024]{1,0:T(8,128)(2,1)S(1)}, s32[1,512]{1,0:T(1,128)S(1)}) custom-call(s32[1,512]{1,0:T(1,128)S(1)} %bitcast.12, bf16[512,1024]{1,0:T(8,128)(2,1)S(1)} %copy-done), custom_call_target="tpu_custom_call" | custom-call | tf_op jit(solution)/shard_map/place/pallas_call | solution.py:116
  3.8 41.8 %all_to_all.16 = bf16[128,8,1024]{2,1,0:T(8,128)(2,1)S(1)} all-to-all(bf16[128,8,1024]{2,1,0:T(8,128)(2,1)S(1)} %bitcast.9), channel_id=1, replica_groups=mesh['work'=128] {'work'}, dimensions={0} | all-to-all | bytes 4194304 | tf_op jit(solution)/shard_map/all_to_all | solution.py:109
  45.6 2.7 %maxima.1 = f32[128,128]{1,0:T(8,128)S(1)} custom-call(bf16[1024,1024]{1,0:T(8,128)(2,1)S(1)} %bitcast.8), custom_call_target="tpu_custom_call" | custom-call | tf_op jit(solution)/shard_map/maxima/pallas_call | solution.py:122
  48.3 13.4 %all_to_all.17 = f32[128,1,128]{2,1,0:T(1,128)S(1)} all-to-all(f32[128,1,128]{2,1,0:T(1,128)S(1)} %bitcast.10), channel_id=1, replica_groups=mesh['work'=128] {'work'}, dimensions={0} | all-to-all | bytes 131072 | tf_op jit(solution)/shard_map/all_to_all | solution.py:109
  61.7 0.8 %lookup.1 = f32[1,512]{1,0:T(1,128)} custom-call(s32[1,512]{1,0:T(1,128)S(1)} %get-tuple-element.7.slot_ref, f32[128,128]{1,0:T(8,128)S(1)} %bitcast.11), custom_call_target="tpu_custom_call" | custom-call | tf_op jit(solution)/shard_map/lookup/pallas_call | solution.py:124
Async XLA Ops:
  0.0 1.2 %copy-start = (bf16[512,1024]{1,0:T(8,128)(2,1)S(1)}, bf16[512,1024]{1,0:T(8,128)(2,1)}, u32[]{:S(2)}) copy-start(bf16[512,1024]{1,0:T(8,128)(2,1)} %rows_ref.1) | copy-start | bytes 3145732
  1.2 0.7 %copy-start.1 = (s32[512,1]{0,1:T(1,128)S(1)}, s32[512,1]{0,1:T(1,128)}, u32[]{:S(2)}) copy-start(s32[512,1]{0,1:T(1,128)} %param.3) | copy-start | bytes 6148

commit v2 on v1

v2 whole, which is shorter than its diff:
```python
import jax
import jax.numpy as jnp
from jax import lax
from jax.experimental import pallas as pl
from jax.experimental.pallas import tpu as pltpu
from jax.sharding import PartitionSpec as P

CLUSTERS = 256
CL_DEV = 2
MOST = 4
PART = CL_DEV * MOST
DEAD = 4.0
LOW = -1e30
CHUNKS = 4
PARAMS = pltpu.CompilerParams(vmem_limit_bytes=40 * 1024 * 1024)


def iota(shape, dim):
    return lax.broadcasted_iota(jnp.int32, shape, dim)


def parts_of(values):
    out = []
    for _ in range(2):
        part = values.astype(jnp.bfloat16)
        out.append(part)
        values = values - part.astype(jnp.float32)
    return out


def bits(mask):
    return mask.astype(jnp.float32).astype(jnp.bfloat16)


def dot(a, b, dims):
    return lax.dot_general(a, b, (dims, ((), ())), preferred_element_type=jnp.float32)


def place_kernel(label_hbm, rows_hbm, send_ref, slot_ref, label_ref, rows_ref, unit_ref, chosen_ref, label_sem, rows_sem):
    rows = rows_ref.shape[0]
    total = send_ref.shape[0]
    chunk = rows // CHUNKS
    label_copy = pltpu.make_async_copy(label_hbm, label_ref, label_sem)
    label_copy.start()
    copies = []
    for index in range(CHUNKS):
        part = pl.ds(index * chunk, chunk)
        copies.append(pltpu.make_async_copy(rows_hbm.at[part], rows_ref.at[part], rows_sem.at[index]))
        copies[-1].start()
    before = bits(iota((rows, rows), 0) < iota((rows, rows), 1))
    label_copy.wait()
    label = label_ref[...]
    member = iota((CLUSTERS, rows), 0) == label
    earlier = dot(bits(member), before, ((1,), (0,)))
    rank = jnp.sum(jnp.where(member, earlier, 0.0), axis=0, keepdims=True)
    slot = label * MOST + rank.astype(jnp.int32)
    slot_ref[...] = slot
    step = 256
    empty = []
    for first in range(0, total, step):
        chosen = (iota((step, rows), 0) + first == slot).astype(jnp.float32)
        empty.append(DEAD - DEAD * jnp.sum(chosen, axis=1, keepdims=True))
        chosen_ref[first : first + step, :] = chosen.astype(jnp.bfloat16)
    for index in range(CHUNKS):
        part = pl.ds(index * chunk, chunk)
        copies[index].wait()
        values = rows_ref[part, :].astype(jnp.float32)
        squares = jnp.sum(values * values, axis=1, keepdims=True)
        unit_ref[part, :] = (values * lax.rsqrt(squares + 1e-06)).astype(jnp.bfloat16)
    for first in range(0, total, step):
        placed = dot(chosen_ref[first : first + step, :], unit_ref[...], ((1,), (0,)))
        send_ref[first : first + step, :128] = (placed[:, :128] + empty[first // step]).astype(jnp.bfloat16)
        send_ref[first : first + step, 128:] = placed[:, 128:].astype(jnp.bfloat16)


def maxima_kernel(rows_ref, out_ref):
    total = rows_ref.shape[0]
    count = total // PART
    step = 256
    blocks = total // step
    tile = 128
    same = (iota((step, tile), 0) & MOST) == (iota((step, tile), 1) & MOST)
    other = iota((step, step), 0) != iota((step, step), 1)
    empty = [rows_ref[b * step : (b + 1) * step, :tile].astype(jnp.float32) for b in range(blocks)]
    down = [jnp.where(same & (e[:, :1] < 0.5 * DEAD), 0.0, LOW) for e in empty]
    across = [jnp.where(jnp.transpose(e)[:1] < 0.5 * DEAD, 0.0, LOW) for e in empty]
    over_rows = [jnp.full((8, step), -1.0, jnp.float32) for _ in range(blocks)]
    over_columns = [jnp.full((step, tile), -1.0, jnp.float32) for _ in range(blocks)]
    for i in range(blocks):
        for j in range(i, blocks):
            sim = dot(rows_ref[i * step : (i + 1) * step, :], rows_ref[j * step : (j + 1) * step, :], ((1,), (1,)))
            sim = sim + jnp.concatenate([down[i]] * (step // tile), axis=1)
            if i == j:
                sim = jnp.where(other, sim, LOW)
            else:
                sim = sim + across[j]
                for left in range(0, step, tile):
                    over_columns[i] = jnp.maximum(over_columns[i], sim[:, left : left + tile])
            over_rows[j] = jnp.maximum(over_rows[j], jnp.max(sim.reshape(step // 8, 8, step), axis=0))
    best = jnp.max(jnp.concatenate(over_rows, axis=1), axis=0, keepdims=True)
    rest = jnp.max(jnp.concatenate(over_columns, axis=0), axis=1, keepdims=True)
    mine = iota((count, total), 1) // PART == iota((count, total), 0)
    spread = iota((total, tile), 0) % PART == iota((total, tile), 1) % PART
    mine_one, spread_one = bits(mine), bits(spread)
    one = jnp.zeros((count, tile), jnp.float32)
    for piece in parts_of(best):
        one = one + dot(jnp.where(mine, piece.astype(jnp.float32), 0.0).astype(jnp.bfloat16), spread_one, ((1,), (0,)))
    two = jnp.zeros((count, tile), jnp.float32)
    for piece in parts_of(rest):
        two = two + dot(mine_one, jnp.where(spread, piece.astype(jnp.float32), 0.0).astype(jnp.bfloat16), ((1,), (0,)))
    out_ref[...] = jnp.maximum(one, two)


def lookup_kernel(slot_ref, found_ref, out_ref):
    rows = slot_ref.shape[1]
    count = found_ref.shape[0]
    slot = slot_ref[...]
    owner = bits(iota((count, rows), 0) == slot // PART)
    picked = jnp.zeros((128, rows), jnp.float32)
    for piece in parts_of(found_ref[...]):
        picked = picked + dot(piece, owner, ((0,), (0,)))
    picked = picked[:PART]
    out_ref[...] = jnp.sum(jnp.where(iota((PART, rows), 0) == slot % PART, picked, 0.0), axis=0, keepdims=True)


def call(kernel, out_shape, name):
    return pl.pallas_call(
        kernel,
        out_shape=out_shape,
        compiler_params=PARAMS,
        name=name,
    )


def exchange(array):
    return lax.all_to_all(array, "work", split_axis=0, concat_axis=0, tiled=True)


def local(embeddings, labels):
    count = lax.axis_size("work")
    rows, width = embeddings.shape
    total = count * PART
    send, slot = pl.pallas_call(
        place_kernel,
        out_shape=(jax.ShapeDtypeStruct((total, width), jnp.bfloat16), jax.ShapeDtypeStruct((1, rows), jnp.int32)),
        in_specs=[pl.BlockSpec(memory_space=pltpu.HBM)] * 2,
        scratch_shapes=[
            pltpu.VMEM((1, rows), jnp.int32),
            pltpu.VMEM((rows, width), jnp.bfloat16),
            pltpu.VMEM((rows, width), jnp.bfloat16),
            pltpu.VMEM((total, rows), jnp.bfloat16),
            pltpu.SemaphoreType.DMA,
            pltpu.SemaphoreType.DMA((CHUNKS,)),
        ],
        compiler_params=pltpu.CompilerParams(vmem_limit_bytes=40 * 1024 * 1024),
        name="place",
    )(
        pltpu.with_memory_space_constraint(labels.reshape(1, rows), pltpu.HBM),
        pltpu.with_memory_space_constraint(embeddings, pltpu.HBM),
    )
    held = exchange(send.reshape(count, PART, width)).reshape(total, width)
    best = call(maxima_kernel, jax.ShapeDtypeStruct((count, 128), jnp.float32), "maxima")(held)
    found = exchange(best)
    nearest = call(lookup_kernel, jax.ShapeDtypeStruct((1, rows), jnp.float32), "lookup")(slot, found)
    return nearest.reshape(rows)


def solution(mesh):
    return jax.shard_map(
        local,
        mesh=mesh,
        in_specs=(P("work", None), P("work", None)),
        out_specs=P("work"),
        check_vma=False,
    )
```

time: 62.8 us -> 61.6 us (0.981)
  local copies, waits for them, and re-layouts: 1.91 us -> 0 us
  Pallas kernels: 5.44 us -> 6.18 us
    unnamed x4 -> x0, local copies, waits for them, and re-layouts: 1.91 us -> none
    pallas_call x1, Pallas kernels: 1.89 us -> 3.38 us  [local(): pl.pallas_call(place_kernel, out_shape=(jax.ShapeDtypeStruct((total, widt...]
    pallas_call x1, Pallas kernels: 2.7 us -> 1.99 us  [local(): call(maxima_kernel, jax.ShapeDtypeStruct((count, 128), jnp.float32), 'max...]
where the time goes in v2:
time: 61.6 us; the launch traced here: 61.5 us
  blocking collectives  55.3 us (90%)
  Pallas kernels  6.18 us (10%)
    all_to_all x2, blocking collectives, exchange(): lax.all_to_all(array, 'work', split_axis=0, concat_axis=0, tiled=True)  55.3 us
    pallas_call x1, Pallas kernels, local(): pl.pallas_call(place_kernel, out_shape=(jax.ShapeDtypeStruct((total, widt...  3.38 us
    pallas_call x1, Pallas kernels, local(): call(maxima_kernel, jax.ShapeDtypeStruct((count, 128), jnp.float32), 'max...  1.99 us

profile of v2, /device:TPU:1, one launch (start us, length us, event | category | flops | bytes accessed | tf_op | source)
XLA Modules:
  0.0 61.5 jit_solution(4098187054551884544)
XLA Ops:
  0.0 3.4 %place.1 = (bf16[1024,1024]{1,0:T(8,128)(2,1)S(1)}, s32[1,512]{1,0:T(1,128)S(1)}) custom-call(s32[1,512]{1,0:T(1,128)} %bitcast.12, bf16[512,1024]{1,0:T(8,128)(2,1)} %rows_hbm.1), custom_call_target="tpu_custom_call" | custom-call | tf_op jit(solution)/shard_map/place/pallas_call | solution.py:143
  3.4 41.8 %all_to_all.16 = bf16[128,8,1024]{2,1,0:T(8,128)(2,1)S(1)} all-to-all(bf16[128,8,1024]{2,1,0:T(8,128)(2,1)S(1)} %bitcast.9), channel_id=1, replica_groups=mesh['work'=128] {'work'}, dimensions={0} | all-to-all | bytes 4194304 | tf_op jit(solution)/shard_map/all_to_all | solution.py:136
  45.2 2.0 %maxima.1 = f32[128,128]{1,0:T(8,128)S(1)} custom-call(bf16[1024,1024]{1,0:T(8,128)(2,1)S(1)} %bitcast.8), custom_call_target="tpu_custom_call" | custom-call | tf_op jit(solution)/shard_map/maxima/pallas_call | solution.py:162
  47.2 13.4 %all_to_all.17 = f32[128,1,128]{2,1,0:T(1,128)S(1)} all-to-all(f32[128,1,128]{2,1,0:T(1,128)S(1)} %bitcast.10), channel_id=1, replica_groups=mesh['work'=128] {'work'}, dimensions={0} | all-to-all | bytes 131072 | tf_op jit(solution)/shard_map/all_to_all | solution.py:136
  60.7 0.8 %lookup.1 = f32[1,512]{1,0:T(1,128)} custom-call(s32[1,512]{1,0:T(1,128)S(1)} %get-tuple-element.7.slot_ref, f32[128,128]{1,0:T(8,128)S(1)} %bitcast.11), custom_call_target="tpu_custom_call" | custom-call | tf_op jit(solution)/shard_map/lookup/pallas_call | solution.py:164

commit v3 on v2

--- a/solution.py
+++ b/solution.py
@@ -9,9 +9,9 @@
 CL_DEV = 2
 MOST = 4
 PART = CL_DEV * MOST
-DEAD = 4.0
+MARK = 2.0**-126
 LOW = -1e30
-CHUNKS = 4
+CHUNKS = 1
 PARAMS = pltpu.CompilerParams(vmem_limit_bytes=40 * 1024 * 1024)
 
 
@@ -56,21 +56,25 @@
     slot = label * MOST + rank.astype(jnp.int32)
     slot_ref[...] = slot
     step = 256
-    empty = []
     for first in range(0, total, step):
-        chosen = (iota((step, rows), 0) + first == slot).astype(jnp.float32)
-        empty.append(DEAD - DEAD * jnp.sum(chosen, axis=1, keepdims=True))
-        chosen_ref[first : first + step, :] = chosen.astype(jnp.bfloat16)
+        chosen_ref[first : first + step, :] = bits(iota((step, rows), 0) + first == slot)
+    first_lane = iota((chunk, 128), 1) == 0
     for index in range(CHUNKS):
         part = pl.ds(index * chunk, chunk)
         copies[index].wait()
         values = rows_ref[part, :].astype(jnp.float32)
-        squares = jnp.sum(values * values, axis=1, keepdims=True)
-        unit_ref[part, :] = (values * lax.rsqrt(squares + 1e-06)).astype(jnp.bfloat16)
-    for first in range(0, total, step):
-        placed = dot(chosen_ref[first : first + step, :], unit_ref[...], ((1,), (0,)))
-        send_ref[first : first + step, :128] = (placed[:, :128] + empty[first // step]).astype(jnp.bfloat16)
-        send_ref[first : first + step, 128:] = placed[:, 128:].astype(jnp.bfloat16)
+        squares = values * values
+        folded = squares[:, :128]
+        for left in range(128, rows_ref.shape[1], 128):
+            folded = folded + squares[:, left : left + 128]
+        squares = jnp.sum(folded, axis=1, keepdims=True)
+        unit = values * lax.rsqrt(squares + 1e-06)
+        head = unit[:, :128]
+        unit_ref[part, :128] = jnp.where((jnp.abs(head) < MARK) & first_lane, MARK, head).astype(jnp.bfloat16)
+        unit_ref[part, 128:] = unit[:, 128:].astype(jnp.bfloat16)
+    for left in range(0, rows_ref.shape[1], step):
+        placed = dot(chosen_ref[...], unit_ref[:, left : left + step], ((1,), (0,)))
+        send_ref[:, left : left + step] = placed.astype(jnp.bfloat16)
 
 
 def maxima_kernel(rows_ref, out_ref):
@@ -82,8 +86,8 @@
     same = (iota((step, tile), 0) & MOST) == (iota((step, tile), 1) & MOST)
     other = iota((step, step), 0) != iota((step, step), 1)
     empty = [rows_ref[b * step : (b + 1) * step, :tile].astype(jnp.float32) for b in range(blocks)]
-    down = [jnp.where(same & (e[:, :1] < 0.5 * DEAD), 0.0, LOW) for e in empty]
-    across = [jnp.where(jnp.transpose(e)[:1] < 0.5 * DEAD, 0.0, LOW) for e in empty]
+    down = [jnp.where(same & (e[:, :1] != 0.0), 0.0, LOW) for e in empty]
+    across = [jnp.where(jnp.transpose(e)[:1] != 0.0, 0.0, LOW) for e in empty]
     over_rows = [jnp.full((8, step), -1.0, jnp.float32) for _ in range(blocks)]
     over_columns = [jnp.full((step, tile), -1.0, jnp.float32) for _ in range(blocks)]
     for i in range(blocks):
@@ -97,18 +101,14 @@
                 for left in range(0, step, tile):
                     over_columns[i] = jnp.maximum(over_columns[i], sim[:, left : left + tile])
             over_rows[j] = jnp.maximum(over_rows[j], jnp.max(sim.reshape(step // 8, 8, step), axis=0))
-    best = jnp.max(jnp.concatenate(over_rows, axis=1), axis=0, keepdims=True)
-    rest = jnp.max(jnp.concatenate(over_columns, axis=0), axis=1, keepdims=True)
-    mine = iota((count, total), 1) // PART == iota((count, total), 0)
-    spread = iota((total, tile), 0) % PART == iota((total, tile), 1) % PART
-    mine_one, spread_one = bits(mine), bits(spread)
-    one = jnp.zeros((count, tile), jnp.float32)
-    for piece in parts_of(best):
-        one = one + dot(jnp.where(mine, piece.astype(jnp.float32), 0.0).astype(jnp.bfloat16), spread_one, ((1,), (0,)))
-    two = jnp.zeros((count, tile), jnp.float32)
-    for piece in parts_of(rest):
-        two = two + dot(mine_one, jnp.where(spread, piece.astype(jnp.float32), 0.0).astype(jnp.bfloat16), ((1,), (0,)))
-    out_ref[...] = jnp.maximum(one, two)
+    best = []
+    for over_row, over_column in zip(over_rows, over_columns):
+        column = jnp.max(jnp.transpose(over_column), axis=0, keepdims=True)
+        best.append(jnp.maximum(jnp.max(over_row, axis=0, keepdims=True), column))
+    best = jnp.concatenate(best, axis=1)
+    best = jnp.concatenate([best[:, left : left + tile] for left in range(0, total, tile)], axis=0)
+    for place in range(tile // PART):
+        out_ref[pl.ds(place, total // tile, stride=tile // PART), :] = pltpu.roll(best, -place * PART % tile, axis=1)
 
 
 def lookup_kernel(slot_ref, found_ref, out_ref):

time: 61.6 us -> 60.8 us (0.987)
  Pallas kernels: 6.18 us -> 5.41 us
where the time goes in v3:
time: 60.8 us; the launch traced here: 60.7 us
  blocking collectives  55.2 us (91%)
  Pallas kernels  5.41 us (9%)
    all_to_all x2, blocking collectives, exchange(): lax.all_to_all(array, 'work', split_axis=0, concat_axis=0, tiled=True)  55.2 us
    pallas_call x1, Pallas kernels, local(): pl.pallas_call(place_kernel, out_shape=(jax.ShapeDtypeStruct((total, widt...  2.82 us
    pallas_call x1, Pallas kernels, local(): call(maxima_kernel, jax.ShapeDtypeStruct((count, 128), jnp.float32), 'max...  1.79 us

profile of v3, /device:TPU:1, one launch (start us, length us, event | category | flops | bytes accessed | tf_op | source)
XLA Modules:
  0.0 60.7 jit_solution(13473472685800576706)
XLA Ops:
  0.0 2.8 %place.1 = (bf16[1024,1024]{1,0:T(8,128)(2,1)S(1)}, s32[1,512]{1,0:T(1,128)S(1)}) custom-call(s32[1,512]{1,0:T(1,128)} %bitcast.12, bf16[512,1024]{1,0:T(8,128)(2,1)} %rows_hbm.1), custom_call_target="tpu_custom_call" | custom-call | tf_op jit(solution)/shard_map/place/pallas_call | solution.py:143
  2.8 41.8 %all_to_all.16 = bf16[128,8,1024]{2,1,0:T(8,128)(2,1)S(1)} all-to-all(bf16[128,8,1024]{2,1,0:T(8,128)(2,1)S(1)} %bitcast.9), channel_id=1, replica_groups=mesh['work'=128] {'work'}, dimensions={0} | all-to-all | bytes 4194304 | tf_op jit(solution)/shard_map/all_to_all | solution.py:136
  44.6 1.8 %maxima.1 = f32[128,128]{1,0:T(8,128)S(1)} custom-call(bf16[1024,1024]{1,0:T(8,128)(2,1)S(1)} %bitcast.8), custom_call_target="tpu_custom_call" | custom-call | tf_op jit(solution)/shard_map/maxima/pallas_call | solution.py:162
  46.4 13.4 %all_to_all.17 = f32[128,1,128]{2,1,0:T(1,128)S(1)} all-to-all(f32[128,1,128]{2,1,0:T(1,128)S(1)} %bitcast.10), channel_id=1, replica_groups=mesh['work'=128] {'work'}, dimensions={0} | all-to-all | bytes 131072 | tf_op jit(solution)/shard_map/all_to_all | solution.py:136
  59.9 0.8 %lookup.1 = f32[1,512]{1,0:T(1,128)} custom-call(s32[1,512]{1,0:T(1,128)S(1)} %get-tuple-element.7.slot_ref, f32[128,128]{1,0:T(8,128)S(1)} %bitcast.11), custom_call_target="tpu_custom_call" | custom-call | tf_op jit(solution)/shard_map/lookup/pallas_call | solution.py:164

commit v4 on v3

--- a/solution.py
+++ b/solution.py
@@ -53,7 +53,7 @@
     member = iota((CLUSTERS, rows), 0) == label
     earlier = dot(bits(member), before, ((1,), (0,)))
     rank = jnp.sum(jnp.where(member, earlier, 0.0), axis=0, keepdims=True)
-    slot = label * MOST + rank.astype(jnp.int32)
+    slot = (label * MOST + rank.astype(jnp.int32)) ^ ((lax.axis_index("work") & 2) * (MOST // 2))
     slot_ref[...] = slot
     step = 256
     for first in range(0, total, step):
@@ -77,38 +77,51 @@
         send_ref[:, left : left + step] = placed.astype(jnp.bfloat16)
 
 
-def maxima_kernel(rows_ref, out_ref):
-    total = rows_ref.shape[0]
-    count = total // PART
+def maxima_kernel(rows_ref, out_ref, left_ref, right_ref):
+    total, width = rows_ref.shape
+    half = total // CL_DEV
     step = 256
-    blocks = total // step
+    blocks = half // step
     tile = 128
-    same = (iota((step, tile), 0) & MOST) == (iota((step, tile), 1) & MOST)
+    upper = iota((16, width), 0) & MOST == 0
+    for group in range(total // 32):
+        one = rows_ref[group * 32 : group * 32 + 16, :]
+        two = rows_ref[group * 32 + 16 : group * 32 + 32, :]
+        left_ref[group * 16 : group * 16 + 16, :] = jnp.where(upper, one, two)
+        right_ref[group * 16 : group * 16 + 16, :] = jnp.where(upper, two, one)
     other = iota((step, step), 0) != iota((step, step), 1)
-    empty = [rows_ref[b * step : (b + 1) * step, :tile].astype(jnp.float32) for b in range(blocks)]
-    down = [jnp.where(same & (e[:, :1] != 0.0), 0.0, LOW) for e in empty]
-    across = [jnp.where(jnp.transpose(e)[:1] != 0.0, 0.0, LOW) for e in empty]
-    over_rows = [jnp.full((8, step), -1.0, jnp.float32) for _ in range(blocks)]
-    over_columns = [jnp.full((step, tile), -1.0, jnp.float32) for _ in range(blocks)]
-    for i in range(blocks):
-        for j in range(i, blocks):
-            sim = dot(rows_ref[i * step : (i + 1) * step, :], rows_ref[j * step : (j + 1) * step, :], ((1,), (1,)))
-            sim = sim + jnp.concatenate([down[i]] * (step // tile), axis=1)
-            if i == j:
-                sim = jnp.where(other, sim, LOW)
-            else:
-                sim = sim + across[j]
-                for left in range(0, step, tile):
-                    over_columns[i] = jnp.maximum(over_columns[i], sim[:, left : left + tile])
-            over_rows[j] = jnp.maximum(over_rows[j], jnp.max(sim.reshape(step // 8, 8, step), axis=0))
-    best = []
-    for over_row, over_column in zip(over_rows, over_columns):
-        column = jnp.max(jnp.transpose(over_column), axis=0, keepdims=True)
-        best.append(jnp.maximum(jnp.max(over_row, axis=0, keepdims=True), column))
-    best = jnp.concatenate(best, axis=1)
-    best = jnp.concatenate([best[:, left : left + tile] for left in range(0, total, tile)], axis=0)
+    found = []
+    for held in (left_ref, right_ref):
+        mark = [held[b * step : (b + 1) * step, :tile].astype(jnp.float32) for b in range(blocks)]
+        down = [jnp.where(m[:, :1] != 0.0, 0.0, LOW) for m in mark]
+        across = [jnp.where(jnp.transpose(m)[:1] != 0.0, 0.0, LOW) for m in mark]
+        over_rows = [jnp.full((8, step), -1.0, jnp.float32) for _ in range(blocks)]
+        over_columns = [jnp.full((step, tile), -1.0, jnp.float32) for _ in range(blocks)]
+        for i in range(blocks):
+            for j in range(i, blocks):
+                sim = dot(held[i * step : (i + 1) * step, :], held[j * step : (j + 1) * step, :], ((1,), (1,)))
+                sim = sim + down[i]
+                if i == j:
+                    sim = jnp.where(other, sim, LOW)
+                else:
+                    sim = sim + across[j]
+                    for first in range(0, step, tile):
+                        over_columns[i] = jnp.maximum(over_columns[i], sim[:, first : first + tile])
+                over_rows[j] = jnp.maximum(over_rows[j], jnp.max(sim.reshape(step // 8, 8, step), axis=0))
+        best = []
+        for over_row, over_column in zip(over_rows, over_columns):
+            column = jnp.max(jnp.transpose(over_column), axis=0, keepdims=True)
+            best.append(jnp.maximum(jnp.max(over_row, axis=0, keepdims=True), column))
+        best = jnp.concatenate(best, axis=1)
+        found.append(jnp.concatenate([best[:, first : first + tile] for first in range(0, half, tile)], axis=0))
+    first_half = iota(found[0].shape, 1) & MOST == 0
+    best = jnp.concatenate([jnp.where(first_half, found[0], found[1]), jnp.where(first_half, found[1], found[0])], axis=0)
+    lines = half // tile
     for place in range(tile // PART):
-        out_ref[pl.ds(place, total // tile, stride=tile // PART), :] = pltpu.roll(best, -place * PART % tile, axis=1)
+        turned = pltpu.roll(best, -place * PART % tile, axis=1)
+        row = place // 2 * 4 + place % 2
+        out_ref[pl.ds(row, lines, stride=32), :] = turned[:lines]
+        out_ref[pl.ds(row + 2, lines, stride=32), :] = turned[lines:]
 
 
 def lookup_kernel(slot_ref, found_ref, out_ref):
@@ -159,7 +172,13 @@
         pltpu.with_memory_space_constraint(embeddings, pltpu.HBM),
     )
     held = exchange(send.reshape(count, PART, width)).reshape(total, width)
-    best = call(maxima_kernel, jax.ShapeDtypeStruct((count, 128), jnp.float32), "maxima")(held)
+    best = pl.pallas_call(
+        maxima_kernel,
+        out_shape=jax.ShapeDtypeStruct((count, 128), jnp.float32),
+        scratch_shapes=[pltpu.VMEM((total // CL_DEV, width), jnp.bfloat16)] * CL_DEV,
+        compiler_params=PARAMS,
+        name="maxima",
+    )(held)
     found = exchange(best)
     nearest = call(lookup_kernel, jax.ShapeDtypeStruct((1, rows), jnp.float32), "lookup")(slot, found)
     return nearest.reshape(rows)

time: 60.8 us -> 60.4 us (level)
  no operation moved by 1% of the time
where the time goes in v4:
time: 60.4 us; the launch traced here: 60.3 us
  blocking collectives  55.2 us (91%)
  Pallas kernels  4.99 us (8%)
    all_to_all x2, blocking collectives, exchange(): lax.all_to_all(array, 'work', split_axis=0, concat_axis=0, tiled=True)  55.2 us
    pallas_call x1, Pallas kernels, local(): pl.pallas_call(place_kernel, out_shape=(jax.ShapeDtypeStruct((total, widt...  2.82 us
    pallas_call x1, Pallas kernels, local(): pl.pallas_call(maxima_kernel, out_shape=jax.ShapeDtypeStruct((count, 128)...  1.36 us

profile of v4, /device:TPU:1, one launch (start us, length us, event | category | flops | bytes accessed | tf_op | source)
XLA Modules:
  0.0 60.3 jit_solution(1199956629302665038)
XLA Ops:
  0.0 2.8 %place.1 = (bf16[1024,1024]{1,0:T(8,128)(2,1)S(1)}, s32[1,512]{1,0:T(1,128)S(1)}) custom-call(s32[1,512]{1,0:T(1,128)} %bitcast.12, bf16[512,1024]{1,0:T(8,128)(2,1)} %rows_hbm.1), custom_call_target="tpu_custom_call" | custom-call | tf_op jit(solution)/shard_map/place/pallas_call | solution.py:156
  2.8 41.8 %all_to_all.16 = bf16[128,8,1024]{2,1,0:T(8,128)(2,1)S(1)} all-to-all(bf16[128,8,1024]{2,1,0:T(8,128)(2,1)S(1)} %bitcast.9), channel_id=1, replica_groups=mesh['work'=128] {'work'}, dimensions={0} | all-to-all | bytes 4194304 | tf_op jit(solution)/shard_map/all_to_all | solution.py:149
  44.6 1.4 %maxima.1 = f32[128,128]{1,0:T(8,128)S(1)} custom-call(bf16[1024,1024]{1,0:T(8,128)(2,1)S(1)} %bitcast.8), custom_call_target="tpu_custom_call" | custom-call | tf_op jit(solution)/shard_map/maxima/pallas_call | solution.py:175
  46.0 13.4 %all_to_all.17 = f32[128,1,128]{2,1,0:T(1,128)S(1)} all-to-all(f32[128,1,128]{2,1,0:T(1,128)S(1)} %bitcast.10), channel_id=1, replica_groups=mesh['work'=128] {'work'}, dimensions={0} | all-to-all | bytes 131072 | tf_op jit(solution)/shard_map/all_to_all | solution.py:149
  59.4 0.8 %lookup.1 = f32[1,512]{1,0:T(1,128)} custom-call(s32[1,512]{1,0:T(1,128)S(1)} %get-tuple-element.7.slot_ref, f32[128,128]{1,0:T(8,128)S(1)} %bitcast.11), custom_call_target="tpu_custom_call" | custom-call | tf_op jit(solution)/shard_map/lookup/pallas_call | solution.py:183

commit v5 on v4

--- a/solution.py
+++ b/solution.py
@@ -79,6 +79,7 @@
 
 def maxima_kernel(rows_ref, out_ref, left_ref, right_ref):
     total, width = rows_ref.shape
+    count = out_ref.shape[0]
     half = total // CL_DEV
     step = 256
     blocks = half // step
@@ -112,16 +113,16 @@
         for over_row, over_column in zip(over_rows, over_columns):
             column = jnp.max(jnp.transpose(over_column), axis=0, keepdims=True)
             best.append(jnp.maximum(jnp.max(over_row, axis=0, keepdims=True), column))
-        best = jnp.concatenate(best, axis=1)
-        found.append(jnp.concatenate([best[:, first : first + tile] for first in range(0, half, tile)], axis=0))
+        tiles = [row[:, first : first + tile] for row in best for first in range(0, step, tile)]
+        found.append(jnp.concatenate([t for row in tiles for t in (row, pltpu.roll(row, tile // 2, axis=1))], axis=0))
     first_half = iota(found[0].shape, 1) & MOST == 0
-    best = jnp.concatenate([jnp.where(first_half, found[0], found[1]), jnp.where(first_half, found[1], found[0])], axis=0)
-    lines = half // tile
-    for place in range(tile // PART):
-        turned = pltpu.roll(best, -place * PART % tile, axis=1)
-        row = place // 2 * 4 + place % 2
-        out_ref[pl.ds(row, lines, stride=32), :] = turned[:lines]
-        out_ref[pl.ds(row + 2, lines, stride=32), :] = turned[lines:]
+    lines = found[0].shape[0]
+    apart = count // lines
+    for swap in range(CL_DEV):
+        best = jnp.where(first_half, found[swap], found[1 - swap])
+        for place in range(tile // 2 // PART):
+            row = place // 2 * 4 + swap * 2 + place % 2
+            out_ref[pl.ds(row, lines, stride=apart), :] = pltpu.roll(best, -place * PART % tile, axis=1)
 
 
 def lookup_kernel(slot_ref, found_ref, out_ref):

time: 60.4 us -> 60.4 us (level)
  no operation moved by 1% of the time
where the time goes in v5:
time: 60.4 us; the launch traced here: 60.3 us
  blocking collectives  55.2 us (91%)
  Pallas kernels  5.02 us (8%)
    all_to_all x2, blocking collectives, exchange(): lax.all_to_all(array, 'work', split_axis=0, concat_axis=0, tiled=True)  55.2 us
    pallas_call x1, Pallas kernels, local(): pl.pallas_call(place_kernel, out_shape=(jax.ShapeDtypeStruct((total, widt...  2.82 us
    pallas_call x1, Pallas kernels, local(): pl.pallas_call(maxima_kernel, out_shape=jax.ShapeDtypeStruct((count, 128)...  1.39 us

profile of v5, /device:TPU:1, one launch (start us, length us, event | category | flops | bytes accessed | tf_op | source)
XLA Modules:
  0.0 60.3 jit_solution(1516940731827391380)
XLA Ops:
  0.0 2.8 %place.1 = (bf16[1024,1024]{1,0:T(8,128)(2,1)S(1)}, s32[1,512]{1,0:T(1,128)S(1)}) custom-call(s32[1,512]{1,0:T(1,128)} %bitcast.12, bf16[512,1024]{1,0:T(8,128)(2,1)} %rows_hbm.1), custom_call_target="tpu_custom_call" | custom-call | tf_op jit(solution)/shard_map/place/pallas_call | solution.py:157
  2.8 41.8 %all_to_all.16 = bf16[128,8,1024]{2,1,0:T(8,128)(2,1)S(1)} all-to-all(bf16[128,8,1024]{2,1,0:T(8,128)(2,1)S(1)} %bitcast.9), channel_id=1, replica_groups=mesh['work'=128] {'work'}, dimensions={0} | all-to-all | bytes 4194304 | tf_op jit(solution)/shard_map/all_to_all | solution.py:150
  44.6 1.4 %maxima.1 = f32[128,128]{1,0:T(8,128)S(1)} custom-call(bf16[1024,1024]{1,0:T(8,128)(2,1)S(1)} %bitcast.8), custom_call_target="tpu_custom_call" | custom-call | tf_op jit(solution)/shard_map/maxima/pallas_call | solution.py:176
  46.0 13.4 %all_to_all.17 = f32[128,1,128]{2,1,0:T(1,128)S(1)} all-to-all(f32[128,1,128]{2,1,0:T(1,128)S(1)} %bitcast.10), channel_id=1, replica_groups=mesh['work'=128] {'work'}, dimensions={0} | all-to-all | bytes 131072 | tf_op jit(solution)/shard_map/all_to_all | solution.py:150
  59.5 0.8 %lookup.1 = f32[1,512]{1,0:T(1,128)} custom-call(s32[1,512]{1,0:T(1,128)S(1)} %get-tuple-element.7.slot_ref, f32[128,128]{1,0:T(8,128)S(1)} %bitcast.11), custom_call_target="tpu_custom_call" | custom-call | tf_op jit(solution)/shard_map/lookup/pallas_call | solution.py:184

commit v6 on v5

--- a/solution.py
+++ b/solution.py
@@ -11,7 +11,6 @@
 PART = CL_DEV * MOST
 MARK = 2.0**-126
 LOW = -1e30
-CHUNKS = 1
 PARAMS = pltpu.CompilerParams(vmem_limit_bytes=40 * 1024 * 1024)
 
 
@@ -39,14 +38,10 @@
 def place_kernel(label_hbm, rows_hbm, send_ref, slot_ref, label_ref, rows_ref, unit_ref, chosen_ref, label_sem, rows_sem):
     rows = rows_ref.shape[0]
     total = send_ref.shape[0]
-    chunk = rows // CHUNKS
     label_copy = pltpu.make_async_copy(label_hbm, label_ref, label_sem)
     label_copy.start()
-    copies = []
-    for index in range(CHUNKS):
-        part = pl.ds(index * chunk, chunk)
-        copies.append(pltpu.make_async_copy(rows_hbm.at[part], rows_ref.at[part], rows_sem.at[index]))
-        copies[-1].start()
+    rows_copy = pltpu.make_async_copy(rows_hbm, rows_ref, rows_sem)
+    rows_copy.start()
     before = bits(iota((rows, rows), 0) < iota((rows, rows), 1))
     label_copy.wait()
     label = label_ref[...]
@@ -58,26 +53,22 @@
     step = 256
     for first in range(0, total, step):
         chosen_ref[first : first + step, :] = bits(iota((step, rows), 0) + first == slot)
-    first_lane = iota((chunk, 128), 1) == 0
-    for index in range(CHUNKS):
-        part = pl.ds(index * chunk, chunk)
-        copies[index].wait()
-        values = rows_ref[part, :].astype(jnp.float32)
-        squares = values * values
-        folded = squares[:, :128]
-        for left in range(128, rows_ref.shape[1], 128):
-            folded = folded + squares[:, left : left + 128]
-        squares = jnp.sum(folded, axis=1, keepdims=True)
-        unit = values * lax.rsqrt(squares + 1e-06)
-        head = unit[:, :128]
-        unit_ref[part, :128] = jnp.where((jnp.abs(head) < MARK) & first_lane, MARK, head).astype(jnp.bfloat16)
-        unit_ref[part, 128:] = unit[:, 128:].astype(jnp.bfloat16)
+    rows_copy.wait()
+    folded = jnp.zeros((rows, 128), jnp.float32)
+    for left in range(0, rows_ref.shape[1], 128):
+        values = rows_ref[:, left : left + 128].astype(jnp.float32)
+        folded = folded + values * values
+    scale = lax.rsqrt(jnp.sum(folded, axis=1, keepdims=True) + 1e-06)
     for left in range(0, rows_ref.shape[1], step):
+        unit = rows_ref[:, left : left + step].astype(jnp.float32) * scale
+        if left == 0:
+            unit = jnp.where((jnp.abs(unit) < MARK) & (iota(unit.shape, 1) == 0), MARK, unit)
+        unit_ref[:, left : left + step] = unit.astype(jnp.bfloat16)
         placed = dot(chosen_ref[...], unit_ref[:, left : left + step], ((1,), (0,)))
         send_ref[:, left : left + step] = placed.astype(jnp.bfloat16)
 
 
-def maxima_kernel(rows_ref, out_ref, left_ref, right_ref):
+def maxima_kernel(rows_ref, out_ref):
     total, width = rows_ref.shape
     count = out_ref.shape[0]
     half = total // CL_DEV
@@ -85,14 +76,15 @@
     blocks = half // step
     tile = 128
     upper = iota((16, width), 0) & MOST == 0
-    for group in range(total // 32):
-        one = rows_ref[group * 32 : group * 32 + 16, :]
-        two = rows_ref[group * 32 + 16 : group * 32 + 32, :]
-        left_ref[group * 16 : group * 16 + 16, :] = jnp.where(upper, one, two)
-        right_ref[group * 16 : group * 16 + 16, :] = jnp.where(upper, two, one)
+    groups = [rows_ref[first : first + 16, :] for first in range(0, total, 16)]
+    pairs = list(zip(groups[::2], groups[1::2]))
+    sides = [
+        jnp.concatenate([jnp.where(upper, one, two) for one, two in pairs], axis=0),
+        jnp.concatenate([jnp.where(upper, two, one) for one, two in pairs], axis=0),
+    ]
     other = iota((step, step), 0) != iota((step, step), 1)
     found = []
-    for held in (left_ref, right_ref):
+    for held in sides:
         mark = [held[b * step : (b + 1) * step, :tile].astype(jnp.float32) for b in range(blocks)]
         down = [jnp.where(m[:, :1] != 0.0, 0.0, LOW) for m in mark]
         across = [jnp.where(jnp.transpose(m)[:1] != 0.0, 0.0, LOW) for m in mark]
@@ -130,10 +122,9 @@
     count = found_ref.shape[0]
     slot = slot_ref[...]
     owner = bits(iota((count, rows), 0) == slot // PART)
-    picked = jnp.zeros((128, rows), jnp.float32)
-    for piece in parts_of(found_ref[...]):
-        picked = picked + dot(piece, owner, ((0,), (0,)))
-    picked = picked[:PART]
+    found = jnp.concatenate(parts_of(jnp.transpose(found_ref[...])[:PART]), axis=0)
+    picked = dot(found, owner, ((1,), (0,)))
+    picked = picked[:PART] + picked[PART:]
     out_ref[...] = jnp.sum(jnp.where(iota((PART, rows), 0) == slot % PART, picked, 0.0), axis=0, keepdims=True)
 
 
@@ -164,22 +155,16 @@
             pltpu.VMEM((rows, width), jnp.bfloat16),
             pltpu.VMEM((total, rows), jnp.bfloat16),
             pltpu.SemaphoreType.DMA,
-            pltpu.SemaphoreType.DMA((CHUNKS,)),
+            pltpu.SemaphoreType.DMA,
         ],
-        compiler_params=pltpu.CompilerParams(vmem_limit_bytes=40 * 1024 * 1024),
+        compiler_params=PARAMS,
         name="place",
     )(
         pltpu.with_memory_space_constraint(labels.reshape(1, rows), pltpu.HBM),
         pltpu.with_memory_space_constraint(embeddings, pltpu.HBM),
     )
     held = exchange(send.reshape(count, PART, width)).reshape(total, width)
-    best = pl.pallas_call(
-        maxima_kernel,
-        out_shape=jax.ShapeDtypeStruct((count, 128), jnp.float32),
-        scratch_shapes=[pltpu.VMEM((total // CL_DEV, width), jnp.bfloat16)] * CL_DEV,
-        compiler_params=PARAMS,
-        name="maxima",
-    )(held)
+    best = call(maxima_kernel, jax.ShapeDtypeStruct((count, 128), jnp.float32), "maxima")(held)
     found = exchange(best)
     nearest = call(lookup_kernel, jax.ShapeDtypeStruct((1, rows), jnp.float32), "lookup")(slot, found)
     return nearest.reshape(rows)

time: 60.4 us -> 60.3 us (level)
  no operation moved by 1% of the time
where the time goes in v6:
time: 60.3 us; the launch traced here: 60.1 us
  blocking collectives  55.2 us (92%)
  Pallas kernels  4.86 us (8%)
    all_to_all x2, blocking collectives, exchange(): lax.all_to_all(array, 'work', split_axis=0, concat_axis=0, tiled=True)  55.2 us
    pallas_call x1, Pallas kernels, local(): pl.pallas_call(place_kernel, out_shape=(jax.ShapeDtypeStruct((total, widt...  2.77 us
    pallas_call x1, Pallas kernels, local(): call(maxima_kernel, jax.ShapeDtypeStruct((count, 128), jnp.float32), 'max...  1.31 us

profile of v6, /device:TPU:1, one launch (start us, length us, event | category | flops | bytes accessed | tf_op | source)
XLA Modules:
  0.0 60.1 jit_solution(5956987180568796499)
XLA Ops:
  0.0 2.8 %place.1 = (bf16[1024,1024]{1,0:T(8,128)(2,1)S(1)}, s32[1,512]{1,0:T(1,128)S(1)}) custom-call(s32[1,512]{1,0:T(1,128)} %bitcast.12, bf16[512,1024]{1,0:T(8,128)(2,1)} %rows_hbm.1), custom_call_target="tpu_custom_call" | custom-call | tf_op jit(solution)/shard_map/place/pallas_call | solution.py:148
  2.8 41.8 %all_to_all.16 = bf16[128,8,1024]{2,1,0:T(8,128)(2,1)S(1)} all-to-all(bf16[128,8,1024]{2,1,0:T(8,128)(2,1)S(1)} %bitcast.9), channel_id=1, replica_groups=mesh['work'=128] {'work'}, dimensions={0} | all-to-all | bytes 4194304 | tf_op jit(solution)/shard_map/all_to_all | solution.py:141
  44.6 1.3 %maxima.1 = f32[128,128]{1,0:T(8,128)S(1)} custom-call(bf16[1024,1024]{1,0:T(8,128)(2,1)S(1)} %bitcast.8), custom_call_target="tpu_custom_call" | custom-call | tf_op jit(solution)/shard_map/maxima/pallas_call | solution.py:167
  45.9 13.4 %all_to_all.17 = f32[128,1,128]{2,1,0:T(1,128)S(1)} all-to-all(f32[128,1,128]{2,1,0:T(1,128)S(1)} %bitcast.10), channel_id=1, replica_groups=mesh['work'=128] {'work'}, dimensions={0} | all-to-all | bytes 131072 | tf_op jit(solution)/shard_map/all_to_all | solution.py:141
  59.3 0.8 %lookup.1 = f32[1,512]{1,0:T(1,128)} custom-call(s32[1,512]{1,0:T(1,128)S(1)} %get-tuple-element.7.slot_ref, f32[128,128]{1,0:T(8,128)S(1)} %bitcast.11), custom_call_target="tpu_custom_call" | custom-call | tf_op jit(solution)/shard_map/lookup/pallas_call | solution.py:169

commit v7 on v6

--- a/solution.py
+++ b/solution.py
@@ -35,7 +35,7 @@
     return lax.dot_general(a, b, (dims, ((), ())), preferred_element_type=jnp.float32)
 
 
-def place_kernel(label_hbm, rows_hbm, send_ref, slot_ref, label_ref, rows_ref, unit_ref, chosen_ref, label_sem, rows_sem):
+def place_kernel(label_hbm, rows_hbm, send_ref, slot_ref, label_ref, rows_ref, chosen_ref, label_sem, rows_sem):
     rows = rows_ref.shape[0]
     total = send_ref.shape[0]
     label_copy = pltpu.make_async_copy(label_hbm, label_ref, label_sem)
@@ -54,17 +54,11 @@
     for first in range(0, total, step):
         chosen_ref[first : first + step, :] = bits(iota((step, rows), 0) + first == slot)
     rows_copy.wait()
-    folded = jnp.zeros((rows, 128), jnp.float32)
-    for left in range(0, rows_ref.shape[1], 128):
-        values = rows_ref[:, left : left + 128].astype(jnp.float32)
-        folded = folded + values * values
-    scale = lax.rsqrt(jnp.sum(folded, axis=1, keepdims=True) + 1e-06)
+    head = rows_ref[:, :128].astype(jnp.float32)
+    head = jnp.where((jnp.abs(head) < MARK) & (iota(head.shape, 1) == 0), MARK, head)
+    rows_ref[:, :128] = head.astype(jnp.bfloat16)
     for left in range(0, rows_ref.shape[1], step):
-        unit = rows_ref[:, left : left + step].astype(jnp.float32) * scale
-        if left == 0:
-            unit = jnp.where((jnp.abs(unit) < MARK) & (iota(unit.shape, 1) == 0), MARK, unit)
-        unit_ref[:, left : left + step] = unit.astype(jnp.bfloat16)
-        placed = dot(chosen_ref[...], unit_ref[:, left : left + step], ((1,), (0,)))
+        placed = dot(chosen_ref[...], rows_ref[:, left : left + step], ((1,), (0,)))
         send_ref[:, left : left + step] = placed.astype(jnp.bfloat16)
 
 
@@ -88,23 +82,29 @@
         mark = [held[b * step : (b + 1) * step, :tile].astype(jnp.float32) for b in range(blocks)]
         down = [jnp.where(m[:, :1] != 0.0, 0.0, LOW) for m in mark]
         across = [jnp.where(jnp.transpose(m)[:1] != 0.0, 0.0, LOW) for m in mark]
-        over_rows = [jnp.full((8, step), -1.0, jnp.float32) for _ in range(blocks)]
-        over_columns = [jnp.full((step, tile), -1.0, jnp.float32) for _ in range(blocks)]
+        sims = {}
         for i in range(blocks):
             for j in range(i, blocks):
-                sim = dot(held[i * step : (i + 1) * step, :], held[j * step : (j + 1) * step, :], ((1,), (1,)))
-                sim = sim + down[i]
-                if i == j:
-                    sim = jnp.where(other, sim, LOW)
-                else:
-                    sim = sim + across[j]
-                    for first in range(0, step, tile):
-                        over_columns[i] = jnp.maximum(over_columns[i], sim[:, first : first + tile])
-                over_rows[j] = jnp.maximum(over_rows[j], jnp.max(sim.reshape(step // 8, 8, step), axis=0))
+                sims[i, j] = dot(held[i * step : (i + 1) * step, :], held[j * step : (j + 1) * step, :], ((1,), (1,)))
+        own = [jnp.where(other, 0.0, sims[b, b]) for b in range(blocks)]
+        scale_down = [lax.rsqrt(jnp.sum(o, axis=1, keepdims=True) + 1e-06) for o in own]
+        scale_across = [lax.rsqrt(jnp.sum(o, axis=0, keepdims=True) + 1e-06) for o in own]
+        over_rows = [jnp.full((8, step), LOW, jnp.float32) for _ in range(blocks)]
+        over_columns = [jnp.full((step, tile), LOW, jnp.float32) for _ in range(blocks)]
+        for i, j in sims:
+            sim = sims[i, j] * scale_down[i] + down[i]
+            if i == j:
+                sim = jnp.where(other, sim, LOW)
+            else:
+                turned = sims[i, j] * scale_across[j] + across[j]
+                for first in range(0, step, tile):
+                    over_columns[i] = jnp.maximum(over_columns[i], turned[:, first : first + tile])
+            over_rows[j] = jnp.maximum(over_rows[j], jnp.max(sim.reshape(step // 8, 8, step), axis=0))
         best = []
-        for over_row, over_column in zip(over_rows, over_columns):
+        for over_row, over_column, scale in zip(over_rows, over_columns, scale_across):
             column = jnp.max(jnp.transpose(over_column), axis=0, keepdims=True)
-            best.append(jnp.maximum(jnp.max(over_row, axis=0, keepdims=True), column))
+            row = jnp.maximum(jnp.max(over_row, axis=0, keepdims=True), column)
+            best.append(jnp.maximum(row * scale, -1.0))
         tiles = [row[:, first : first + tile] for row in best for first in range(0, step, tile)]
         found.append(jnp.concatenate([t for row in tiles for t in (row, pltpu.roll(row, tile // 2, axis=1))], axis=0))
     first_half = iota(found[0].shape, 1) & MOST == 0
@@ -152,7 +152,6 @@
         scratch_shapes=[
             pltpu.VMEM((1, rows), jnp.int32),
             pltpu.VMEM((rows, width), jnp.bfloat16),
-            pltpu.VMEM((rows, width), jnp.bfloat16),
             pltpu.VMEM((total, rows), jnp.bfloat16),
             pltpu.SemaphoreType.DMA,
             pltpu.SemaphoreType.DMA,

time: 60.3 us -> 60.2 us (level)
  no operation moved by 1% of the time
where the time goes in v7:
time: 60.2 us; the launch traced here: 60 us
  blocking collectives  55.2 us (92%)
  Pallas kernels  4.74 us (8%)
    all_to_all x2, blocking collectives, exchange(): lax.all_to_all(array, 'work', split_axis=0, concat_axis=0, tiled=True)  55.2 us
    pallas_call x1, Pallas kernels, local(): pl.pallas_call(place_kernel, out_shape=(jax.ShapeDtypeStruct((total, widt...  2.54 us
    pallas_call x1, Pallas kernels, local(): call(maxima_kernel, jax.ShapeDtypeStruct((count, 128), jnp.float32), 'max...  1.41 us

profile of v7, /device:TPU:1, one launch (start us, length us, event | category | flops | bytes accessed | tf_op | source)
XLA Modules:
  0.0 60.0 jit_solution(4062349604027662836)
XLA Ops:
  0.0 2.5 %place.1 = (bf16[1024,1024]{1,0:T(8,128)(2,1)S(1)}, s32[1,512]{1,0:T(1,128)S(1)}) custom-call(s32[1,512]{1,0:T(1,128)} %bitcast.12, bf16[512,1024]{1,0:T(8,128)(2,1)} %rows_hbm.1), custom_call_target="tpu_custom_call" | custom-call | tf_op jit(solution)/shard_map/place/pallas_call | solution.py:148
  2.6 41.8 %all_to_all.16 = bf16[128,8,1024]{2,1,0:T(8,128)(2,1)S(1)} all-to-all(bf16[128,8,1024]{2,1,0:T(8,128)(2,1)S(1)} %bitcast.9), channel_id=1, replica_groups=mesh['work'=128] {'work'}, dimensions={0} | all-to-all | bytes 4194304 | tf_op jit(solution)/shard_map/all_to_all | solution.py:141
  44.4 1.4 %maxima.1 = f32[128,128]{1,0:T(8,128)S(1)} custom-call(bf16[1024,1024]{1,0:T(8,128)(2,1)S(1)} %bitcast.8), custom_call_target="tpu_custom_call" | custom-call | tf_op jit(solution)/shard_map/maxima/pallas_call | solution.py:166
  45.8 13.4 %all_to_all.17 = f32[128,1,128]{2,1,0:T(1,128)S(1)} all-to-all(f32[128,1,128]{2,1,0:T(1,128)S(1)} %bitcast.10), channel_id=1, replica_groups=mesh['work'=128] {'work'}, dimensions={0} | all-to-all | bytes 131072 | tf_op jit(solution)/shard_map/all_to_all | solution.py:141
  59.2 0.8 %lookup.1 = f32[1,512]{1,0:T(1,128)} custom-call(s32[1,512]{1,0:T(1,128)S(1)} %get-tuple-element.7.slot_ref, f32[128,128]{1,0:T(8,128)S(1)} %bitcast.11), custom_call_target="tpu_custom_call" | custom-call | tf_op jit(solution)/shard_map/lookup/pallas_call | solution.py:168

commit v8 on v6

--- a/solution.py
+++ b/solution.py
@@ -90,10 +90,10 @@
         across = [jnp.where(jnp.transpose(m)[:1] != 0.0, 0.0, LOW) for m in mark]
         over_rows = [jnp.full((8, step), -1.0, jnp.float32) for _ in range(blocks)]
         over_columns = [jnp.full((step, tile), -1.0, jnp.float32) for _ in range(blocks)]
-        for i in range(blocks):
-            for j in range(i, blocks):
-                sim = dot(held[i * step : (i + 1) * step, :], held[j * step : (j + 1) * step, :], ((1,), (1,)))
-                sim = sim + down[i]
+        for j in reversed(range(blocks)):
+            tall = dot(held[: (j + 1) * step, :], held[j * step : (j + 1) * step, :], ((1,), (1,)))
+            for i in range(j + 1):
+                sim = tall[i * step : (i + 1) * step] + down[i]
                 if i == j:
                     sim = jnp.where(other, sim, LOW)
                 else:

time: 60.3 us -> 60.2 us (level)
  no operation moved by 1% of the time
where the time goes in v8:
time: 60.2 us; the launch traced here: 60 us
  blocking collectives  55.2 us (92%)
  Pallas kernels  4.75 us (8%)
    all_to_all x2, blocking collectives, exchange(): lax.all_to_all(array, 'work', split_axis=0, concat_axis=0, tiled=True)  55.2 us
    pallas_call x1, Pallas kernels, local(): pl.pallas_call(place_kernel, out_shape=(jax.ShapeDtypeStruct((total, widt...  2.77 us

profile of v8, /device:TPU:1, one launch (start us, length us, event | category | flops | bytes accessed | tf_op | source)
XLA Modules:
  0.0 60.0 jit_solution(15576280813882552873)
XLA Ops:
  0.0 2.8 %place.1 = (bf16[1024,1024]{1,0:T(8,128)(2,1)S(1)}, s32[1,512]{1,0:T(1,128)S(1)}) custom-call(s32[1,512]{1,0:T(1,128)} %bitcast.12, bf16[512,1024]{1,0:T(8,128)(2,1)} %rows_hbm.1), custom_call_target="tpu_custom_call" | custom-call | tf_op jit(solution)/shard_map/place/pallas_call | solution.py:148
  2.8 41.8 %all_to_all.16 = bf16[128,8,1024]{2,1,0:T(8,128)(2,1)S(1)} all-to-all(bf16[128,8,1024]{2,1,0:T(8,128)(2,1)S(1)} %bitcast.9), channel_id=1, replica_groups=mesh['work'=128] {'work'}, dimensions={0} | all-to-all | bytes 4194304 | tf_op jit(solution)/shard_map/all_to_all | solution.py:141
  44.6 1.2 %maxima.1 = f32[128,128]{1,0:T(8,128)S(1)} custom-call(bf16[1024,1024]{1,0:T(8,128)(2,1)S(1)} %bitcast.8), custom_call_target="tpu_custom_call" | custom-call | tf_op jit(solution)/shard_map/maxima/pallas_call | solution.py:167
  45.8 13.4 %all_to_all.17 = f32[128,1,128]{2,1,0:T(1,128)S(1)} all-to-all(f32[128,1,128]{2,1,0:T(1,128)S(1)} %bitcast.10), channel_id=1, replica_groups=mesh['work'=128] {'work'}, dimensions={0} | all-to-all | bytes 131072 | tf_op jit(solution)/shard_map/all_to_all | solution.py:141
  59.2 0.8 %lookup.1 = f32[1,512]{1,0:T(1,128)} custom-call(s32[1,512]{1,0:T(1,128)S(1)} %get-tuple-element.7.slot_ref, f32[128,128]{1,0:T(8,128)S(1)} %bitcast.11), custom_call_target="tpu_custom_call" | custom-call | tf_op jit(solution)/shard_map/lookup/pallas_call | solution.py:169

commit v9 on v8

--- a/solution.py
+++ b/solution.py
@@ -87,7 +87,7 @@
     for held in sides:
         mark = [held[b * step : (b + 1) * step, :tile].astype(jnp.float32) for b in range(blocks)]
         down = [jnp.where(m[:, :1] != 0.0, 0.0, LOW) for m in mark]
-        across = [jnp.where(jnp.transpose(m)[:1] != 0.0, 0.0, LOW) for m in mark]
+        across = [jnp.where(jnp.transpose(m)[:1] != 0.0, 0.0, LOW) if b else None for b, m in enumerate(mark)]
         over_rows = [jnp.full((8, step), -1.0, jnp.float32) for _ in range(blocks)]
         over_columns = [jnp.full((step, tile), -1.0, jnp.float32) for _ in range(blocks)]
         for j in reversed(range(blocks)):
@@ -102,9 +102,11 @@
                         over_columns[i] = jnp.maximum(over_columns[i], sim[:, first : first + tile])
                 over_rows[j] = jnp.maximum(over_rows[j], jnp.max(sim.reshape(step // 8, 8, step), axis=0))
         best = []
-        for over_row, over_column in zip(over_rows, over_columns):
-            column = jnp.max(jnp.transpose(over_column), axis=0, keepdims=True)
-            best.append(jnp.maximum(jnp.max(over_row, axis=0, keepdims=True), column))
+        for b in range(blocks):
+            row = jnp.max(over_rows[b], axis=0, keepdims=True)
+            if b < blocks - 1:
+                row = jnp.maximum(row, jnp.max(jnp.transpose(over_columns[b]), axis=0, keepdims=True))
+            best.append(row)
         tiles = [row[:, first : first + tile] for row in best for first in range(0, step, tile)]
         found.append(jnp.concatenate([t for row in tiles for t in (row, pltpu.roll(row, tile // 2, axis=1))], axis=0))
     first_half = iota(found[0].shape, 1) & MOST == 0
@@ -114,7 +116,7 @@
         best = jnp.where(first_half, found[swap], found[1 - swap])
         for place in range(tile // 2 // PART):
             row = place // 2 * 4 + swap * 2 + place % 2
-            out_ref[pl.ds(row, lines, stride=apart), :] = pltpu.roll(best, -place * PART % tile, axis=1)
+            out_ref[pl.ds(row, lines, stride=apart), :] = pltpu.roll(best, -place * PART % tile, axis=1)[:, :PART]
 
 
 def lookup_kernel(slot_ref, found_ref, out_ref):
@@ -122,7 +124,7 @@
     count = found_ref.shape[0]
     slot = slot_ref[...]
     owner = bits(iota((count, rows), 0) == slot // PART)
-    found = jnp.concatenate(parts_of(jnp.transpose(found_ref[...])[:PART]), axis=0)
+    found = jnp.concatenate(parts_of(jnp.transpose(found_ref[...])), axis=0)
     picked = dot(found, owner, ((1,), (0,)))
     picked = picked[:PART] + picked[PART:]
     out_ref[...] = jnp.sum(jnp.where(iota((PART, rows), 0) == slot % PART, picked, 0.0), axis=0, keepdims=True)
@@ -164,7 +166,7 @@
         pltpu.with_memory_space_constraint(embeddings, pltpu.HBM),
     )
     held = exchange(send.reshape(count, PART, width)).reshape(total, width)
-    best = call(maxima_kernel, jax.ShapeDtypeStruct((count, 128), jnp.float32), "maxima")(held)
+    best = call(maxima_kernel, jax.ShapeDtypeStruct((count, PART), jnp.float32), "maxima")(held)
     found = exchange(best)
     nearest = call(lookup_kernel, jax.ShapeDtypeStruct((1, rows), jnp.float32), "lookup")(slot, found)
     return nearest.reshape(rows)

time: 60.2 us -> 60.2 us (level)
  no operation moved by 1% of the time
where the time goes in v9:
time: 60.2 us; the launch traced here: 60 us
  blocking collectives  55.2 us (92%)
  Pallas kernels  4.75 us (8%)
    all_to_all x2, blocking collectives, exchange(): lax.all_to_all(array, 'work', split_axis=0, concat_axis=0, tiled=True)  55.2 us
    pallas_call x1, Pallas kernels, local(): pl.pallas_call(place_kernel, out_shape=(jax.ShapeDtypeStruct((total, widt...  2.77 us

profile of v9, /device:TPU:1, one launch (start us, length us, event | category | flops | bytes accessed | tf_op | source)
XLA Modules:
  0.0 60.0 jit_solution(1379129163326782836)
XLA Ops:
  0.0 2.8 %place.1 = (bf16[1024,1024]{1,0:T(8,128)(2,1)S(1)}, s32[1,512]{1,0:T(1,128)S(1)}) custom-call(s32[1,512]{1,0:T(1,128)} %bitcast.12, bf16[512,1024]{1,0:T(8,128)(2,1)} %rows_hbm.1), custom_call_target="tpu_custom_call" | custom-call | tf_op jit(solution)/shard_map/place/pallas_call | solution.py:150
  2.8 41.8 %all_to_all.16 = bf16[128,8,1024]{2,1,0:T(8,128)(2,1)S(1)} all-to-all(bf16[128,8,1024]{2,1,0:T(8,128)(2,1)S(1)} %bitcast.9), channel_id=1, replica_groups=mesh['work'=128] {'work'}, dimensions={0} | all-to-all | bytes 4194304 | tf_op jit(solution)/shard_map/all_to_all | solution.py:143
  44.6 1.2 %maxima.1 = f32[128,8]{1,0:T(8,128)S(1)} custom-call(bf16[1024,1024]{1,0:T(8,128)(2,1)S(1)} %bitcast.8), custom_call_target="tpu_custom_call" | custom-call | tf_op jit(solution)/shard_map/maxima/pallas_call | solution.py:169
  45.8 13.4 %all_to_all.17 = f32[128,1,8]{2,1,0:T(1,128)S(1)} all-to-all(f32[128,1,8]{2,1,0:T(1,128)S(1)} %bitcast.10), channel_id=1, replica_groups=mesh['work'=128] {'work'}, dimensions={0} | all-to-all | bytes 8192 | tf_op jit(solution)/shard_map/all_to_all | solution.py:143
  59.2 0.8 %lookup.1 = f32[1,512]{1,0:T(1,128)} custom-call(s32[1,512]{1,0:T(1,128)S(1)} %get-tuple-element.7.slot_ref, f32[128,8]{1,0:T(8,128)S(1)} %bitcast.11), custom_call_target="tpu_custom_call" | custom-call | tf_op jit(solution)/shard_map/lookup/pallas_call | solution.py:171

commit v10 on v8

--- a/solution.py
+++ b/solution.py
@@ -59,10 +59,12 @@
         values = rows_ref[:, left : left + 128].astype(jnp.float32)
         folded = folded + values * values
     scale = lax.rsqrt(jnp.sum(folded, axis=1, keepdims=True) + 1e-06)
-    for left in range(0, rows_ref.shape[1], step):
+    for left in reversed(range(0, rows_ref.shape[1], step)):
         unit = rows_ref[:, left : left + step].astype(jnp.float32) * scale
         if left == 0:
-            unit = jnp.where((jnp.abs(unit) < MARK) & (iota(unit.shape, 1) == 0), MARK, unit)
+            head = unit[:, :128]
+            head = jnp.where((jnp.abs(head) < MARK) & (iota(head.shape, 1) == 0), MARK, head)
+            unit = jnp.concatenate([head, unit[:, 128:]], axis=1)
         unit_ref[:, left : left + step] = unit.astype(jnp.bfloat16)
         placed = dot(chosen_ref[...], unit_ref[:, left : left + step], ((1,), (0,)))
         send_ref[:, left : left + step] = placed.astype(jnp.bfloat16)

time: 60.2 us -> 60.2 us (level)
  no operation moved by 1% of the time
where the time goes in v10:
time: 60.2 us; the launch traced here: 60 us
  blocking collectives  55.2 us (92%)
  Pallas kernels  4.73 us (8%)
    all_to_all x2, blocking collectives, exchange(): lax.all_to_all(array, 'work', split_axis=0, concat_axis=0, tiled=True)  55.2 us
    pallas_call x1, Pallas kernels, local(): pl.pallas_call(place_kernel, out_shape=(jax.ShapeDtypeStruct((total, widt...  2.75 us

profile of v10, /device:TPU:1, one launch (start us, length us, event | category | flops | bytes accessed | tf_op | source)
XLA Modules:
  0.0 60.0 jit_solution(9916700437841272374)
XLA Ops:
  0.0 2.7 %place.1 = (bf16[1024,1024]{1,0:T(8,128)(2,1)S(1)}, s32[1,512]{1,0:T(1,128)S(1)}) custom-call(s32[1,512]{1,0:T(1,128)} %bitcast.12, bf16[512,1024]{1,0:T(8,128)(2,1)} %rows_hbm.1), custom_call_target="tpu_custom_call" | custom-call | tf_op jit(solution)/shard_map/place/pallas_call | solution.py:150
  2.8 41.8 %all_to_all.16 = bf16[128,8,1024]{2,1,0:T(8,128)(2,1)S(1)} all-to-all(bf16[128,8,1024]{2,1,0:T(8,128)(2,1)S(1)} %bitcast.9), channel_id=1, replica_groups=mesh['work'=128] {'work'}, dimensions={0} | all-to-all | bytes 4194304 | tf_op jit(solution)/shard_map/all_to_all | solution.py:143
  44.6 1.2 %maxima.1 = f32[128,128]{1,0:T(8,128)S(1)} custom-call(bf16[1024,1024]{1,0:T(8,128)(2,1)S(1)} %bitcast.8), custom_call_target="tpu_custom_call" | custom-call | tf_op jit(solution)/shard_map/maxima/pallas_call | solution.py:169
  45.8 13.4 %all_to_all.17 = f32[128,1,128]{2,1,0:T(1,128)S(1)} all-to-all(f32[128,1,128]{2,1,0:T(1,128)S(1)} %bitcast.10), channel_id=1, replica_groups=mesh['work'=128] {'work'}, dimensions={0} | all-to-all | bytes 131072 | tf_op jit(solution)/shard_map/all_to_all | solution.py:143
  59.2 0.8 %lookup.1 = f32[1,512]{1,0:T(1,128)} custom-call(s32[1,512]{1,0:T(1,128)S(1)} %get-tuple-element.7.slot_ref, f32[128,128]{1,0:T(8,128)S(1)} %bitcast.11), custom_call_target="tpu_custom_call" | custom-call | tf_op jit(solution)/shard_map/lookup/pallas_call | solution.py:171

commit v11 on v10

--- a/solution.py
+++ b/solution.py
@@ -89,7 +89,7 @@
     for held in sides:
         mark = [held[b * step : (b + 1) * step, :tile].astype(jnp.float32) for b in range(blocks)]
         down = [jnp.where(m[:, :1] != 0.0, 0.0, LOW) for m in mark]
-        across = [jnp.where(jnp.transpose(m)[:1] != 0.0, 0.0, LOW) for m in mark]
+        across = [jnp.where(jnp.transpose(m)[:1] != 0.0, 0.0, LOW) if b else None for b, m in enumerate(mark)]
         over_rows = [jnp.full((8, step), -1.0, jnp.float32) for _ in range(blocks)]
         over_columns = [jnp.full((step, tile), -1.0, jnp.float32) for _ in range(blocks)]
         for j in reversed(range(blocks)):
@@ -104,9 +104,11 @@
                         over_columns[i] = jnp.maximum(over_columns[i], sim[:, first : first + tile])
                 over_rows[j] = jnp.maximum(over_rows[j], jnp.max(sim.reshape(step // 8, 8, step), axis=0))
         best = []
-        for over_row, over_column in zip(over_rows, over_columns):
-            column = jnp.max(jnp.transpose(over_column), axis=0, keepdims=True)
-            best.append(jnp.maximum(jnp.max(over_row, axis=0, keepdims=True), column))
+        for b in range(blocks):
+            row = jnp.max(over_rows[b], axis=0, keepdims=True)
+            if b < blocks - 1:
+                row = jnp.maximum(row, jnp.max(jnp.transpose(over_columns[b]), axis=0, keepdims=True))
+            best.append(row)
         tiles = [row[:, first : first + tile] for row in best for first in range(0, step, tile)]
         found.append(jnp.concatenate([t for row in tiles for t in (row, pltpu.roll(row, tile // 2, axis=1))], axis=0))
     first_half = iota(found[0].shape, 1) & MOST == 0

time: 60.2 us -> 60.2 us (level)
  no operation moved by 1% of the time
where the time goes in v11:
time: 60.2 us; the launch traced here: 60 us
  blocking collectives  55.2 us (92%)
  Pallas kernels  4.73 us (8%)
    all_to_all x2, blocking collectives, exchange(): lax.all_to_all(array, 'work', split_axis=0, concat_axis=0, tiled=True)  55.2 us
    pallas_call x1, Pallas kernels, local(): pl.pallas_call(place_kernel, out_shape=(jax.ShapeDtypeStruct((total, widt...  2.75 us

profile of v11, /device:TPU:1, one launch (start us, length us, event | category | flops | bytes accessed | tf_op | source)
XLA Modules:
  0.0 60.0 jit_solution(16294488451458082495)
XLA Ops:
  0.0 2.7 %place.1 = (bf16[1024,1024]{1,0:T(8,128)(2,1)S(1)}, s32[1,512]{1,0:T(1,128)S(1)}) custom-call(s32[1,512]{1,0:T(1,128)} %bitcast.12, bf16[512,1024]{1,0:T(8,128)(2,1)} %rows_hbm.1), custom_call_target="tpu_custom_call" | custom-call | tf_op jit(solution)/shard_map/place/pallas_call | solution.py:152
  2.8 41.8 %all_to_all.16 = bf16[128,8,1024]{2,1,0:T(8,128)(2,1)S(1)} all-to-all(bf16[128,8,1024]{2,1,0:T(8,128)(2,1)S(1)} %bitcast.9), channel_id=1, replica_groups=mesh['work'=128] {'work'}, dimensions={0} | all-to-all | bytes 4194304 | tf_op jit(solution)/shard_map/all_to_all | solution.py:145
  44.6 1.2 %maxima.1 = f32[128,128]{1,0:T(8,128)S(1)} custom-call(bf16[1024,1024]{1,0:T(8,128)(2,1)S(1)} %bitcast.8), custom_call_target="tpu_custom_call" | custom-call | tf_op jit(solution)/shard_map/maxima/pallas_call | solution.py:171
  45.8 13.4 %all_to_all.17 = f32[128,1,128]{2,1,0:T(1,128)S(1)} all-to-all(f32[128,1,128]{2,1,0:T(1,128)S(1)} %bitcast.10), channel_id=1, replica_groups=mesh['work'=128] {'work'}, dimensions={0} | all-to-all | bytes 131072 | tf_op jit(solution)/shard_map/all_to_all | solution.py:145
  59.2 0.8 %lookup.1 = f32[1,512]{1,0:T(1,128)} custom-call(s32[1,512]{1,0:T(1,128)S(1)} %get-tuple-element.7.slot_ref, f32[128,128]{1,0:T(8,128)S(1)} %bitcast.11), custom_call_target="tpu_custom_call" | custom-call | tf_op jit(solution)/shard_map/lookup/pallas_call | solution.py:173
